TPU v7x, 512 devices: a whole 4x8x8 slice. The times are simulated.
512 devices in a mesh: replica: 16 (over y, core), fsdp: 32 (over x, z).
Axes of the slice: x: 4, y: 8, z: 8, core: 2. Of those that a mesh axis runs over, the one named last changes fastest.
Arguments:
- momentum: float32 [16, 256, 14336], P('replica', 'fsdp'), may hold values from -6 to 6
- gradient: bfloat16 [16, 256, 14336], P('replica', 'fsdp'), may hold values from -6 to 6
- selection: int32 [16, 4, 224, 2], replicated, may hold values from 0 to 63, as said below
Outputs:
- residual_momentum: float32 [16, 256, 14336], P('replica', 'fsdp')
- update: float32 [256, 14336], P(None, 'fsdp')
Inputs may be any that keep to these rules, and one draw needn't show every extreme that they name: `selection`: for each replica and span, the 2 block numbers are distinct.
All inputs are finite; a program needn't handle non-finite values.
Results may differ from a plain program's by a relative error of at most 0.0003.
Values sent between devices are 32-bit elements; how exact they have to be, the bound alone decides.
A program may use at most 64 MiB of HBM per device.

v0:
```python
import jax
import jax.numpy as jnp
from jax import lax
from jax.sharding import PartitionSpec as P

SPAN_SIDE = 64
BLOCK_SIDE = 8
BLOCKS_KEPT = 2
decay_rate = 0.9
highest = lax.Precision.HIGHEST


def from_everyone(value, axis):
    size = lax.axis_size(axis)
    return lax.all_to_all(
        jnp.broadcast_to(value[None], (size, *value.shape)), axis, 0, 0, tiled=True
    )


def joined_along(tiles, dim):
    shape = list(tiles.shape[1:])
    shape[dim] *= tiles.shape[0]
    return jnp.moveaxis(tiles, 0, dim).reshape(shape)


def gathered_copies(value, axis, dim):
    tiles = from_everyone(value, axis)
    return joined_along(tiles, dim)


def cosine_table(side):
    freq = jnp.arange(side, dtype=jnp.float32)[:, None]
    place = jnp.arange(side, dtype=jnp.float32)[None, :]
    scale = jnp.where(freq == 0, jnp.sqrt(1.0 / side), jnp.sqrt(2.0 / side))
    return scale * jnp.cos(jnp.pi * (2.0 * place + 1.0) * freq / (2.0 * side))


def side_marks(index):
    per_side = SPAN_SIDE // BLOCK_SIDE
    return (index[..., None] == jnp.arange(per_side, dtype=jnp.int32)).astype(jnp.float32)


def pick_rows(index, tiles):
    return jnp.einsum("...p,pia->...ia", side_marks(index), tiles, precision=highest)


def local(momentum, gradient, selection):
    table = cosine_table(SPAN_SIDE)
    per_side = SPAN_SIDE // BLOCK_SIDE
    tiles = table.reshape(per_side, BLOCK_SIDE, SPAN_SIDE)
    zero = jnp.zeros((), jnp.int32)
    fsdp_count = lax.axis_size("fsdp")
    fsdp_rank = lax.axis_index("fsdp")
    replica_rank = lax.axis_index("replica")
    replicas = selection.shape[0]
    decayed = decay_rate * momentum[0] + gradient[0].astype(jnp.float32)
    rows_dev, width = decayed.shape
    rows_all = rows_dev * fsdp_count
    span_rows = rows_all // SPAN_SIDE
    local_cols = width // fsdp_count
    span_cols = local_cols // SPAN_SIDE
    all_cols = width // SPAN_SIDE
    group = SPAN_SIDE // rows_dev
    span_row_own = fsdp_rank // group
    square = BLOCK_SIDE * BLOCK_SIDE
    column_start = fsdp_rank * span_cols
    chosen_all = lax.dynamic_slice(
        selection, (zero, zero, column_start, zero), (replicas, span_rows, span_cols, BLOCKS_KEPT)
    )
    chosen_own = lax.dynamic_index_in_dim(chosen_all, replica_rank, 0, keepdims=False)
    row_own = pick_rows(chosen_own // per_side, tiles)
    col_own = pick_rows(chosen_own % per_side, tiles)
    mine_all = lax.dynamic_slice(
        selection, (replica_rank, span_row_own, zero, zero), (1, 1, all_cols, BLOCKS_KEPT)
    )
    mine_all = mine_all.reshape(all_cols, BLOCKS_KEPT)
    owned = lax.all_to_all(decayed, "fsdp", split_axis=1, concat_axis=0, tiled=True)
    spans = owned.reshape(span_rows, SPAN_SIDE, span_cols, SPAN_SIDE)
    kept = jnp.einsum("rckia,racb,rckjb->rckij", row_own, spans, col_own, precision=highest)
    kept = kept.reshape(span_rows, span_cols, BLOCKS_KEPT, square)
    packed = kept.reshape(1, span_rows, span_cols, BLOCKS_KEPT * square)
    piece = gathered_copies(packed, "replica", 0)
    count = piece.shape[0]
    values = piece.reshape(count, span_rows, span_cols, BLOCKS_KEPT, BLOCK_SIDE, BLOCK_SIDE)
    row_sel = pick_rows(chosen_all // per_side, tiles)
    col_sel = pick_rows(chosen_all % per_side, tiles)
    summed = jnp.einsum("qrckia,qrckij,qrckjb->racb", row_sel, values, col_sel, precision=highest)
    update = summed.reshape(rows_all, local_cols)
    own_values = kept.reshape(span_rows, span_cols, BLOCKS_KEPT, BLOCK_SIDE, BLOCK_SIDE)
    extracted = jnp.einsum(
        "rckia,rckij,rckjb->racb", row_own, own_values, col_own, precision=highest
    )
    extracted = extracted.reshape(rows_all, local_cols)
    taken = lax.all_to_all(extracted, "fsdp", split_axis=0, concat_axis=1, tiled=True)
    residual_momentum = decayed - taken
    return (residual_momentum[None], update)


def solution(mesh):
    placed = (P("replica", "fsdp", None), P("replica", "fsdp", None), P())
    return jax.shard_map(
        local,
        mesh=mesh,
        in_specs=placed,
        out_specs=(P("replica", "fsdp", None), P(None, "fsdp")),
        check_vma=False,
    )
```

profile of v0, /device:TPU:1, one launch (start us, length us, event | category | flops | bytes accessed | tf_op | source)
XLA Modules:
  0.0 84.9 jit_solution(9852488467808630540)
XLA Ops:
  0.6 1.2 %convert_add_fusion = f32[1,8,14336]{2,1,0:T(8,128)S(1)} fusion(bf16[1,8,14336]{2,1,0:T(8,128)(2,1)} %param.4, f32[1,8,14336]{2,1,0:T(8,128)} %param.3), kind=kLoop, calls=%fused_computation.9 | loop fusion | flops 344064 | bytes 1146880 | tf_op jit(solution)/shard_map/add | solution.py:56
  2.1 1.1 %copy.44 = f32[8,32,448]{2,0,1:T(8,128)} copy(f32[8,32,448]{2,1,0:T(8,128)S(1)} %add.64) | data formatting | bytes 917504 | tf_op jit(solution)/shard_map/add | solution.py:56
  3.2 13.7 %all-to-all-start = ((f32[8,32,448]{2,0,1:T(8,128)}), f32[8,32,448]{2,0,1:T(8,128)S(1)}, u32[]{:S(2)}, u32[]{:S(2)}) async-start(f32[8,32,448]{2,0,1:T(8,128)} %copy.44), calls=%async_computation | async-start | bytes 1048576 | tf_op jit(solution)/shard_map/all_to_all | solution.py:77
  17.7 0.4 fusion.30
  18.2 0.4 fusion.28
  18.6 3.6 %fusion.13 = f32[16,4,7,2,8,64]{5,0,4,3,2,1:T(8,128)} fusion(s32[16,4,7,2]{0,3,2,1:T(2,128)S(1)} %copy.58, f32[8,8]{0,1:T(8,128)S(1)} %multiply_add_fusion, f32[64]{0:T(128)S(1)} %add_multiply_fusion, f32[8,8]{0,1:T(8,128)S(1)} %compare_select_fusion), kind=kOutput, calls=%fused_computation.13 | convolution fusion | flops 44059648 | bytes 1839360 | tf_op jit(solution)/shard_map/...p,pia->...ia/dot_general | solution.py:44
  22.2 9.0 %all-to-all-done = f32[8,32,448]{2,0,1:T(8,128)S(1)} async-done(((f32[8,32,448]{2,0,1:T(8,128)}), f32[8,32,448]{2,0,1:T(8,128)S(1)}, u32[]{:S(2)}, u32[]{:S(2)}) %all-to-all-start) | async-done | bytes 458784 | tf_op jit(solution)/shard_map/all_to_all | solution.py:77
  31.5 1.0 %fusion.10 = f32[4,7,64,2,8]{2,4,3,1,0:T(8,128)S(1)} fusion(f32[4,64,7,64,1]{3,2,1,0,4:T(8,128)S(1)} %bitcast.78, f32[4,7,2,8,64]{4,1,3,2,0:T(8,128)S(1)} %fusion.30), kind=kOutput, calls=%fused_computation.7 | convolution fusion | flops 22020096 | bytes 688128 | tf_op jit(solution)/shard_map/rckia,racb,rckjb->rckij/dot_general | solution.py:79
  32.5 0.5 fusion.19
  33.2 0.7 broadcast_in_dim.15
  33.9 10.6 %all-to-all-start.2 = ((f32[16,1,4,7,128]{4,2,3,1,0:T(4,128)}), f32[16,1,4,7,128]{4,2,3,1,0:T(4,128)S(1)}, u32[]{:S(2)}, u32[]{:S(2)}) async-start(f32[16,1,4,7,128]{4,2,3,1,0:T(4,128)} %broadcast_in_dim.15), calls=%async_computation.2 | async-start | bytes 458752 | tf_op jit(solution)/shard_map/all_to_all | solution.py:15
  44.5 3.6 %fusion.16 = f32[16,4,7,2,8,64]{5,0,4,3,2,1:T(8,128)} fusion(s32[16,4,7,2]{0,3,2,1:T(2,128)S(1)} %copy.61, f32[8,8]{0,1:T(8,128)S(1)} %multiply_add_fusion, f32[64]{0:T(128)S(1)} %add_multiply_fusion, f32[8,8]{0,1:T(8,128)S(1)} %compare_select_fusion), kind=kOutput, calls=%fused_computation.15 | convolution fusion | flops 44059648 | bytes 1839360 | tf_op jit(solution)/shard_map/...p,pia->...ia/dot_general | solution.py:44
  48.1 0.6 fusion.21
  48.7 1.6 %convolution_bitcast_fusion = f32[4,64,7,64]{3,1,2,0:T(8,128)S(1)} fusion(f32[4,7,2,8,64]{4,3,2,1,0:T(8,128)S(1)} %fusion.21, f32[4,7,2,8,64]{4,1,3,2,0:T(8,128)S(1)} %fusion.28), kind=kOutput, calls=%fused_computation.5 | convolution fusion | flops 22020096 | bytes 688128 | tf_op jit(solution)/shard_map/rckia,rckij,rckjb->racb/dot_general | solution.py:90
  50.4 0.5 copy.54
  50.9 1.0 %all_to_all.29 = f32[32,8,448]{2,1,0:T(8,128)} reshape(f32[4,64,7,64]{3,2,1,0:T(8,128)S(1)} %copy.54) | data formatting | bytes 917504 | tf_op jit(solution)/shard_map/all_to_all | solution.py:94
  51.9 3.7 %all-to-all-done.2 = f32[16,1,4,7,128]{4,2,3,1,0:T(4,128)S(1)} async-done(((f32[16,1,4,7,128]{4,2,3,1,0:T(4,128)}), f32[16,1,4,7,128]{4,2,3,1,0:T(4,128)S(1)}, u32[]{:S(2)}, u32[]{:S(2)}) %all-to-all-start.2) | async-done | bytes 229408 | tf_op jit(solution)/shard_map/all_to_all | solution.py:15
  55.6 5.5 %all-to-all-start.1 = ((f32[32,8,448]{2,1,0:T(8,128)}), f32[32,8,448]{2,1,0:T(8,128)S(1)}, u32[]{:S(2)}, u32[]{:S(2)}) async-start(f32[32,8,448]{2,1,0:T(8,128)} %all_to_all.29), calls=%async_computation.1 | async-start | bytes 1048576 | tf_op jit(solution)/shard_map/all_to_all | solution.py:94
  61.1 0.5 copy.57
  61.7 4.1 %copy.73 = f32[16,4,7,2,8,8]{4,5,3,1,2,0:T(8,128)} copy(f32[16,4,7,2,8,8]{0,5,4,3,2,1:T(8,128)S(1)} %bitcast.77) | data formatting | bytes 458752 | tf_op jit(solution)/shard_map/reshape;reshape | solution.py:84
  65.7 9.2 %fusion.2 = f32[16,4,7,2,8,64]{5,4,3,1,2,0:T(8,128)S(1)} fusion(f32[16,4,7,2,8,8]{4,5,3,1,2,0:T(8,128)} %copy.73, f32[16,4,7,2,8,64]{5,0,4,3,2,1:T(8,128)} %fusion.13), kind=kOutput, calls=%fused_computation.2 | convolution fusion | flops 44040192 | bytes 3899392 | tf_op jit(solution)/shard_map/qrckia,qrckij,qrckjb->racb/dot_general | solution.py:87
  75.0 6.9 %fusion.5 = f32[4,64,7,64]{3,1,2,0:T(8,128)S(1)} fusion(f32[16,4,7,2,8,64]{5,0,4,3,2,1:T(8,128)S(1)} %copy-done, f32[16,4,7,2,8,64]{5,4,3,1,2,0:T(8,128)S(1)} %fusion.2), kind=kOutput, calls=%fused_computation.6 | convolution fusion | flops 352321536 | bytes 4128768 | tf_op jit(solution)/shard_map/qrckia,qrckij,qrckjb->racb/dot_general | solution.py:87
  82.2 1.3 %reshape.117 = f32[256,448]{0,1:T(8,128)} reshape(f32[4,64,7,64]{1,0,3,2:T(4,128)S(1)} %copy.64) | data formatting | bytes 917504 | tf_op jit(solution)/shard_map/reshape | solution.py:88
  84.1 0.8 sub.17
  (22 shorter events, 2.2 us)
Async XLA Ops:
  0.6 16.4 %copy-start.1 = (s32[16,4,224,2]{2,3,1,0:T(2,128)S(1)}, s32[16,4,224,2]{2,3,1,0:T(2,128)}, u32[]{:S(2)}) copy-start(s32[16,4,224,2]{2,3,1,0:T(2,128)} %param.5) | copy-start | bytes 344068
  3.2 28.0 %all-to-all-start = ((f32[8,32,448]{2,0,1:T(8,128)}), f32[8,32,448]{2,0,1:T(8,128)S(1)}, u32[]{:S(2)}, u32[]{:S(2)}) async-start(f32[8,32,448]{2,0,1:T(8,128)} %copy.44), calls=%async_computation | async-start | bytes 1048576 | tf_op jit(solution)/shard_map/all_to_all | solution.py:77
  33.9 21.7 %all-to-all-start.2 = ((f32[16,1,4,7,128]{4,2,3,1,0:T(4,128)}), f32[16,1,4,7,128]{4,2,3,1,0:T(4,128)S(1)}, u32[]{:S(2)}, u32[]{:S(2)}) async-start(f32[16,1,4,7,128]{4,2,3,1,0:T(4,128)} %broadcast_in_dim.15), calls=%async_computation.2 | async-start | bytes 458752 | tf_op jit(solution)/shard_map/all_to_all | solution.py:15
  55.6 28.0 %all-to-all-start.1 = ((f32[32,8,448]{2,1,0:T(8,128)}), f32[32,8,448]{2,1,0:T(8,128)S(1)}, u32[]{:S(2)}, u32[]{:S(2)}) async-start(f32[32,8,448]{2,1,0:T(8,128)} %all_to_all.29), calls=%async_computation.1 | async-start | bytes 1048576 | tf_op jit(solution)/shard_map/all_to_all | solution.py:94
  65.7 9.2 %copy-start = (f32[16,4,7,2,8,64]{5,0,4,3,2,1:T(8,128)S(1)}, f32[16,4,7,2,8,64]{5,0,4,3,2,1:T(8,128)}, u32[]{:S(2)}) copy-start(f32[16,4,7,2,8,64]{5,0,4,3,2,1:T(8,128)} %fusion.16) | copy-start | bytes 5505028
where the time goes:
time: 85.4 us; the launch traced here: 84.9 us
  starting transfers between devices  29.9 us (35%)
  matrix products  27.9 us (33%)
  waiting for transfers between devices  12.7 us (15%)
  local copies, waits for them, and re-layouts  11.2 us (13%)
  other arithmetic  2.38 us (3%)
    dot_general x2, matrix products, local(): jnp.einsum('qrckia,qrckij,qrckjb->racb', row_sel, values, col_sel, precis...  16.1 us
    all_to_all x1, starting transfers between devices, local(): lax.all_to_all(decayed, 'fsdp', split_axis=1, concat_axis=0, tiled=True)  13.7 us
    all_to_all x1, starting transfers between devices, from_everyone(): lax.all_to_all(jnp.broadcast_to(value[None], (size, *value.shape)), axis,...  10.6 us
    all_to_all x1, waiting for transfers between devices, local(): lax.all_to_all(decayed, 'fsdp', split_axis=1, concat_axis=0, tiled=True)  9.05 us
    dot_general x4, matrix products, pick_rows(): jnp.einsum('...p,pia->...ia', side_marks(index), tiles, precision=highest)  8.08 us
    all_to_all x1, starting transfers between devices, local(): lax.all_to_all(extracted, 'fsdp', split_axis=0, concat_axis=1, tiled=True)  5.52 us
    another operation x1, local copies, waits for them, and re-layouts, local(): piece.reshape(count, span_rows, span_cols, BLOCKS_KEPT, BLOCK_SIDE, BLOCK...  4.08 us
    all_to_all x1, waiting for transfers between devices, from_everyone(): lax.all_to_all(jnp.broadcast_to(value[None], (size, *value.shape)), axis,...  3.65 us
  transfers between devices with their start and end apart: 3, of which 2 were waited for; matrix products, arithmetic and copies ran while one was open for 40% of the time, Pallas kernels for 0%

commit v1 on v0

--- a/solution.py
+++ b/solution.py
@@ -91,7 +91,12 @@
         "rckia,rckij,rckjb->racb", row_own, own_values, col_own, precision=highest
     )
     extracted = extracted.reshape(rows_all, local_cols)
-    taken = lax.all_to_all(extracted, "fsdp", split_axis=0, concat_axis=1, tiled=True)
+    taken = jnp.concatenate(
+        lax.all_to_all(
+            jnp.stack(jnp.split(extracted, lax.axis_size("fsdp"), axis=0)), "fsdp", 0, 0
+        ),
+        axis=1,
+    )
     residual_momentum = decayed - taken
     return (residual_momentum[None], update)
 

time: 85.4 us -> 132 us (1.55)
  local copies, waits for them, and re-layouts: 11.2 us -> 64.2 us
  waiting for transfers between devices: 12.7 us -> 5.45 us
    another operation x0 -> x35, local copies, waits for them, and re-layouts: none -> 33.8 us  [local(): jnp.stack(jnp.split(extracted, lax.axis_size('fsdp'), axis=0))]
    unnamed x4 -> x65, local copies, waits for them, and re-layouts: 0.01 us -> 18.7 us
    all_to_all x1, waiting for transfers between devices: 3.65 us -> 0.01 us  [from_everyone(): lax.all_to_all(jnp.broadcast_to(value[None], (size, *value.shape)), axis,...]
    all_to_all x1, waiting for transfers between devices: 9.05 us -> 5.44 us  [local(): lax.all_to_all(decayed, 'fsdp', split_axis=1, concat_axis=0, tiled=True)]
    all_to_all x3 -> x0, local copies, waits for them, and re-layouts: 1.55 us -> none  [local(): lax.all_to_all(extracted, 'fsdp', split_axis=0, concat_axis=1, tiled=True)]
  transfers between devices with their start and end apart: 3 -> 3, of which waited for: 2 -> 1; matrix products, arithmetic and copies ran while one was open for 40% -> 38% of each run, Pallas kernels for 0% -> 0%
where the time goes in v1:
time: 132 us; the launch traced here: 131 us
  local copies, waits for them, and re-layouts  64.2 us (49%)
  starting transfers between devices  29.7 us (22%)
  matrix products  28.2 us (21%)
  waiting for transfers between devices  5.45 us (4%)
  other arithmetic  2.38 us (2%)
    another operation x35, local copies, waits for them, and re-layouts, local(): jnp.stack(jnp.split(extracted, lax.axis_size('fsdp'), axis=0))  33.8 us
    unnamed x65, local copies, waits for them, and re-layouts  18.7 us
    dot_general x2, matrix products, local(): jnp.einsum('qrckia,qrckij,qrckjb->racb', row_sel, values, col_sel, precis...  16.3 us
    all_to_all x1, starting transfers between devices, local(): lax.all_to_all(decayed, 'fsdp', split_axis=1, concat_axis=0, tiled=True)  13.7 us
    all_to_all x1, starting transfers between devices, from_everyone(): lax.all_to_all(jnp.broadcast_to(value[None], (size, *value.shape)), axis,...  10.6 us
    dot_general x4, matrix products, pick_rows(): jnp.einsum('...p,pia->...ia', side_marks(index), tiles, precision=highest)  8.09 us
    all_to_all x1, waiting for transfers between devices, local(): lax.all_to_all(decayed, 'fsdp', split_axis=1, concat_axis=0, tiled=True)  5.44 us
    all_to_all x1, starting transfers between devices, local(): lax.all_to_all(jnp.stack(jnp.split(extracted, lax.axis_size('fsdp'), axis...  5.36 us
  transfers between devices with their start and end apart: 3, of which 1 were waited for; matrix products, arithmetic and copies ran while one was open for 38% of the time, Pallas kernels for 0%

profile of v1, /device:TPU:1, one launch (start us, length us, event | category | flops | bytes accessed | tf_op | source)
XLA Modules:
  0.0 130.9 jit_solution(15431540403540028077)
XLA Ops:
  3.2 13.7 %all-to-all-start = ((f32[8,32,448]{2,0,1:T(8,128)}), f32[8,32,448]{2,0,1:T(8,128)S(1)}, u32[]{:S(2)}, u32[]{:S(2)}) async-start(f32[8,32,448]{2,0,1:T(8,128)} %copy.107), calls=%async_computation | async-start | bytes 1048576 | tf_op jit(solution)/shard_map/all_to_all | solution.py:77
  18.6 3.6 %fusion.13 = f32[16,4,7,2,8,64]{5,0,4,3,2,1:T(8,128)} fusion(s32[16,4,7,2]{0,3,2,1:T(2,128)S(1)} %copy.153, f32[8,8]{0,1:T(8,128)S(1)} %multiply_add_fusion, f32[64]{0:T(128)S(1)} %add_multiply_fusion, f32[8,8]{0,1:T(8,128)S(1)} %compare_select_fusion), kind=kOutput, calls=%fused_computation.45 | convolution fusion | flops 44059648 | bytes 1839360 | tf_op jit(solution)/shard_map/...p,pia->...ia/dot_general | solution.py:44
  22.2 3.6 %fusion.16 = f32[16,4,7,2,8,64]{5,0,4,3,2,1:T(8,128)} fusion(s32[16,4,7,2]{0,3,2,1:T(2,128)S(1)} %copy.156, f32[8,8]{0,1:T(8,128)S(1)} %multiply_add_fusion, f32[64]{0:T(128)S(1)} %add_multiply_fusion, f32[8,8]{0,1:T(8,128)S(1)} %compare_select_fusion), kind=kOutput, calls=%fused_computation.47 | convolution fusion | flops 44059648 | bytes 1839360 | tf_op jit(solution)/shard_map/...p,pia->...ia/dot_general | solution.py:44
  25.8 5.4 %all-to-all-done = f32[8,32,448]{2,0,1:T(8,128)S(1)} async-done(((f32[8,32,448]{2,0,1:T(8,128)}), f32[8,32,448]{2,0,1:T(8,128)S(1)}, u32[]{:S(2)}, u32[]{:S(2)}) %all-to-all-start) | async-done | bytes 458784 | tf_op jit(solution)/shard_map/all_to_all | solution.py:77
  33.7 1.6 %convolution_bitcast_fusion = f32[4,64,7,64]{3,1,2,0:T(8,128)S(1)} fusion(f32[4,7,2,8,64]{4,3,2,1,0:T(8,128)S(1)} %fusion.21, f32[4,7,2,8,64]{4,1,3,2,0:T(8,128)S(1)} %fusion.28), kind=kOutput, calls=%fused_computation.5 | convolution fusion | flops 22020096 | bytes 688128 | tf_op jit(solution)/shard_map/rckia,rckij,rckjb->racb/dot_general | solution.py:90
  36.2 2.3 %slice_bitcast_fusion.19 = (f32[1,8,448]{1,2,0:T(8,128)}, f32[1,8,448]{1,2,0:T(8,128)}, f32[1,8,448]{1,2,0:T(8,128)}, f32[1,8,448]{1,2,0:T(8,128)}, f32[1,8,448]...) fusion(f32[256,448]{0,1:T(8,128)S(1)} %reshape.121), kind=kLoop, calls=%fused_computation.29 | loop fusion | bytes 372736 | tf_op jit(solution)/shard_map/stack | solution.py:96
  38.6 2.4 %slice_bitcast_fusion = (f32[1,8,448]{1,2,0:T(8,128)S(1)}, f32[1,8,448]{1,2,0:T(8,128)S(1)}, f32[1,8,448]{1,2,0:T(8,128)S(1)}, f32[1,8,448]{1,2,0:T(8,128)S(1)},...) fusion(f32[256,448]{0,1:T(8,128)S(1)} %reshape.121), kind=kLoop, calls=%fused_computation.10 | loop fusion | bytes 544768 | tf_op jit(solution)/shard_map/stack | solution.py:96
  43.4 1.6 %copy.119 = f32[1,8,448]{2,1,0:T(8,128)} copy(f32[1,8,448]{1,2,0:T(8,128)} %get-tuple-element.32) | data formatting | bytes 28672 | tf_op jit(solution)/shard_map/stack | solution.py:96
  45.0 1.6 %copy.120 = f32[1,8,448]{2,1,0:T(8,128)} copy(f32[1,8,448]{1,2,0:T(8,128)} %get-tuple-element.31) | data formatting | bytes 28672 | tf_op jit(solution)/shard_map/stack | solution.py:96
  46.7 1.6 %copy.121 = f32[1,8,448]{2,1,0:T(8,128)} copy(f32[1,8,448]{1,2,0:T(8,128)} %get-tuple-element.30) | data formatting | bytes 28672 | tf_op jit(solution)/shard_map/stack | solution.py:96
  48.3 1.6 %copy.122 = f32[1,8,448]{2,1,0:T(8,128)} copy(f32[1,8,448]{1,2,0:T(8,128)} %get-tuple-element.29) | data formatting | bytes 28672 | tf_op jit(solution)/shard_map/stack | solution.py:96
  49.9 1.6 %copy.123 = f32[1,8,448]{2,1,0:T(8,128)} copy(f32[1,8,448]{1,2,0:T(8,128)} %get-tuple-element.28) | data formatting | bytes 28672 | tf_op jit(solution)/shard_map/stack | solution.py:96
  51.6 1.6 %copy.124 = f32[1,8,448]{2,1,0:T(8,128)} copy(f32[1,8,448]{1,2,0:T(8,128)} %get-tuple-element.27) | data formatting | bytes 28672 | tf_op jit(solution)/shard_map/stack | solution.py:96
  53.2 1.6 %copy.125 = f32[1,8,448]{2,1,0:T(8,128)} copy(f32[1,8,448]{1,2,0:T(8,128)} %get-tuple-element.26) | data formatting | bytes 28672 | tf_op jit(solution)/shard_map/stack | solution.py:96
  54.8 1.6 %copy.126 = f32[1,8,448]{2,1,0:T(8,128)} copy(f32[1,8,448]{1,2,0:T(8,128)} %get-tuple-element.25) | data formatting | bytes 28672 | tf_op jit(solution)/shard_map/stack | solution.py:96
  56.5 1.6 %copy.127 = f32[1,8,448]{2,1,0:T(8,128)} copy(f32[1,8,448]{1,2,0:T(8,128)} %get-tuple-element.24) | data formatting | bytes 28672 | tf_op jit(solution)/shard_map/stack | solution.py:96
  58.1 1.6 %copy.128 = f32[1,8,448]{2,1,0:T(8,128)} copy(f32[1,8,448]{1,2,0:T(8,128)} %get-tuple-element.23) | data formatting | bytes 28672 | tf_op jit(solution)/shard_map/stack | solution.py:96
  59.7 1.6 %copy.129 = f32[1,8,448]{2,1,0:T(8,128)} copy(f32[1,8,448]{1,2,0:T(8,128)} %get-tuple-element.22) | data formatting | bytes 28672 | tf_op jit(solution)/shard_map/stack | solution.py:96
  61.4 1.6 %copy.130 = f32[1,8,448]{2,1,0:T(8,128)} copy(f32[1,8,448]{1,2,0:T(8,128)} %get-tuple-element.21) | data formatting | bytes 28672 | tf_op jit(solution)/shard_map/stack | solution.py:96
  72.4 10.6 %all-to-all-start.2 = ((f32[16,1,4,7,128]{4,2,3,1,0:T(4,128)}), f32[16,1,4,7,128]{4,2,3,1,0:T(4,128)S(1)}, u32[]{:S(2)}, u32[]{:S(2)}) async-start(f32[16,1,4,7,128]{4,2,3,1,0:T(4,128)} %broadcast_in_dim.15), calls=%async_computation.2 | async-start | bytes 458752 | tf_op jit(solution)/shard_map/all_to_all | solution.py:15
  101.6 5.4 %all-to-all-start.1 = ((f32[32,8,448]{2,1,0:T(8,128)}), f32[32,8,448]{2,1,0:T(8,128)S(1)}, u32[]{:S(2)}, u32[]{:S(2)}) async-start(f32[32,8,448]{2,1,0:T(8,128)} %constant_dynamic-update-slice_fusion), calls=%async_computation.1 | async-start | bytes 1048576 | tf_op jit(solution)/shard_map/all_to_all | solution.py:95
  107.5 4.0 %copy.168 = f32[16,4,7,2,8,8]{4,5,3,1,2,0:T(8,128)} copy(f32[16,4,7,2,8,8]{0,5,4,3,2,1:T(8,128)S(1)} %bitcast.143) | data formatting | bytes 458752 | tf_op jit(solution)/shard_map/reshape;reshape | solution.py:84
  111.5 9.4 %fusion.2 = f32[16,4,7,2,8,64]{5,4,3,1,2,0:T(8,128)S(1)} fusion(f32[16,4,7,2,8,8]{4,5,3,1,2,0:T(8,128)} %copy.168, f32[16,4,7,2,8,64]{5,0,4,3,2,1:T(8,128)} %fusion.13), kind=kOutput, calls=%fused_computation.2 | convolution fusion | flops 44040192 | bytes 3899392 | tf_op jit(solution)/shard_map/qrckia,qrckij,qrckjb->racb/dot_general | solution.py:87
  121.0 6.9 %fusion.5 = f32[4,64,7,64]{3,1,2,0:T(8,128)S(1)} fusion(f32[16,4,7,2,8,64]{5,0,4,3,2,1:T(8,128)S(1)} %copy-done, f32[16,4,7,2,8,64]{5,4,3,1,2,0:T(8,128)S(1)} %fusion.2), kind=kOutput, calls=%fused_computation.6 | convolution fusion | flops 352321536 | bytes 4128768 | tf_op jit(solution)/shard_map/qrckia,qrckij,qrckjb->racb/dot_general | solution.py:87
  (118 shorter events, 41.2 us)
Async XLA Ops:
  0.6 16.4 %copy-start.16 = (s32[16,4,224,2]{2,3,1,0:T(2,128)S(1)}, s32[16,4,224,2]{2,3,1,0:T(2,128)}, u32[]{:S(2)}) copy-start(s32[16,4,224,2]{2,3,1,0:T(2,128)} %param.5) | copy-start | bytes 344068
  3.2 28.0 %all-to-all-start = ((f32[8,32,448]{2,0,1:T(8,128)}), f32[8,32,448]{2,0,1:T(8,128)S(1)}, u32[]{:S(2)}, u32[]{:S(2)}) async-start(f32[8,32,448]{2,0,1:T(8,128)} %copy.107), calls=%async_computation | async-start | bytes 1048576 | tf_op jit(solution)/shard_map/all_to_all | solution.py:77
  40.9 28.5 %copy-start.2 = (f32[1,8,448]{1,2,0:T(8,128)S(1)}, f32[1,8,448]{1,2,0:T(8,128)}, u32[]{:S(2)}) copy-start(f32[1,8,448]{1,2,0:T(8,128)} %get-tuple-element.13) | copy-start | bytes 43012
  41.0 28.6 %copy-start.1 = (f32[1,8,448]{1,2,0:T(8,128)S(1)}, f32[1,8,448]{1,2,0:T(8,128)}, u32[]{:S(2)}) copy-start(f32[1,8,448]{1,2,0:T(8,128)} %get-tuple-element.12) | copy-start | bytes 43012
  41.7 27.6 %copy-start.3 = (f32[1,8,448]{1,2,0:T(8,128)S(1)}, f32[1,8,448]{1,2,0:T(8,128)}, u32[]{:S(2)}) copy-start(f32[1,8,448]{1,2,0:T(8,128)} %get-tuple-element.14) | copy-start | bytes 43012
  69.4 13.6 %copy-start.14 = (f32[1,8,448]{2,1,0:T(8,128)S(1)}, f32[1,8,448]{2,1,0:T(8,128)}, u32[]{:S(2)}) copy-start(f32[1,8,448]{2,1,0:T(8,128)} %copy.119) | copy-start | bytes 43012
  69.4 14.2 %copy-start.15 = (f32[1,8,448]{2,1,0:T(8,128)S(1)}, f32[1,8,448]{2,1,0:T(8,128)}, u32[]{:S(2)}) copy-start(f32[1,8,448]{2,1,0:T(8,128)} %copy.120) | copy-start | bytes 43012
  69.4 14.8 %copy-start.13 = (f32[1,8,448]{2,1,0:T(8,128)S(1)}, f32[1,8,448]{2,1,0:T(8,128)}, u32[]{:S(2)}) copy-start(f32[1,8,448]{2,1,0:T(8,128)} %copy.121) | copy-start | bytes 43012
  69.4 15.4 %copy-start.12 = (f32[1,8,448]{2,1,0:T(8,128)S(1)}, f32[1,8,448]{2,1,0:T(8,128)}, u32[]{:S(2)}) copy-start(f32[1,8,448]{2,1,0:T(8,128)} %copy.122) | copy-start | bytes 43012
  69.4 16.0 %copy-start.11 = (f32[1,8,448]{2,1,0:T(8,128)S(1)}, f32[1,8,448]{2,1,0:T(8,128)}, u32[]{:S(2)}) copy-start(f32[1,8,448]{2,1,0:T(8,128)} %copy.123) | copy-start | bytes 43012
  69.4 16.6 %copy-start.10 = (f32[1,8,448]{2,1,0:T(8,128)S(1)}, f32[1,8,448]{2,1,0:T(8,128)}, u32[]{:S(2)}) copy-start(f32[1,8,448]{2,1,0:T(8,128)} %copy.124) | copy-start | bytes 43012
  69.4 17.2 %copy-start.9 = (f32[1,8,448]{2,1,0:T(8,128)S(1)}, f32[1,8,448]{2,1,0:T(8,128)}, u32[]{:S(2)}) copy-start(f32[1,8,448]{2,1,0:T(8,128)} %copy.125) | copy-start | bytes 43012
  69.4 17.8 %copy-start.8 = (f32[1,8,448]{2,1,0:T(8,128)S(1)}, f32[1,8,448]{2,1,0:T(8,128)}, u32[]{:S(2)}) copy-start(f32[1,8,448]{2,1,0:T(8,128)} %copy.126) | copy-start | bytes 43012
  69.4 18.4 %copy-start.7 = (f32[1,8,448]{2,1,0:T(8,128)S(1)}, f32[1,8,448]{2,1,0:T(8,128)}, u32[]{:S(2)}) copy-start(f32[1,8,448]{2,1,0:T(8,128)} %copy.127) | copy-start | bytes 43012
  69.5 18.9 %copy-start.6 = (f32[1,8,448]{2,1,0:T(8,128)S(1)}, f32[1,8,448]{2,1,0:T(8,128)}, u32[]{:S(2)}) copy-start(f32[1,8,448]{2,1,0:T(8,128)} %copy.128) | copy-start | bytes 43012
  69.5 19.5 %copy-start.4 = (f32[1,8,448]{2,1,0:T(8,128)S(1)}, f32[1,8,448]{2,1,0:T(8,128)}, u32[]{:S(2)}) copy-start(f32[1,8,448]{2,1,0:T(8,128)} %copy.129) | copy-start | bytes 43012
  69.5 20.1 %copy-start.5 = (f32[1,8,448]{2,1,0:T(8,128)S(1)}, f32[1,8,448]{2,1,0:T(8,128)}, u32[]{:S(2)}) copy-start(f32[1,8,448]{2,1,0:T(8,128)} %copy.130) | copy-start | bytes 43012
  72.4 29.2 %all-to-all-start.2 = ((f32[16,1,4,7,128]{4,2,3,1,0:T(4,128)}), f32[16,1,4,7,128]{4,2,3,1,0:T(4,128)S(1)}, u32[]{:S(2)}, u32[]{:S(2)}) async-start(f32[16,1,4,7,128]{4,2,3,1,0:T(4,128)} %broadcast_in_dim.15), calls=%async_computation.2 | async-start | bytes 458752 | tf_op jit(solution)/shard_map/all_to_all | solution.py:15
  101.6 27.9 %all-to-all-start.1 = ((f32[32,8,448]{2,1,0:T(8,128)}), f32[32,8,448]{2,1,0:T(8,128)S(1)}, u32[]{:S(2)}, u32[]{:S(2)}) async-start(f32[32,8,448]{2,1,0:T(8,128)} %constant_dynamic-update-slice_fusion), calls=%async_computation.1 | async-start | bytes 1048576 | tf_op jit(solution)/shard_map/all_to_all | solution.py:95
  111.5 9.4 %copy-start = (f32[16,4,7,2,8,64]{5,0,4,3,2,1:T(8,128)S(1)}, f32[16,4,7,2,8,64]{5,0,4,3,2,1:T(8,128)}, u32[]{:S(2)}) copy-start(f32[16,4,7,2,8,64]{5,0,4,3,2,1:T(8,128)} %fusion.16) | copy-start | bytes 5505028
